TPU v7x, 128 devices: a whole 4x4x4 slice. The times are simulated.
128 devices in a mesh: queue: 32 (over y_lo, x, z), tensor: 4 (over y_hi, core).
Axes of the slice: x: 4, y: 4 (y_hi: 2, y_lo: 2; y = y_hi * 2 + y_lo), z: 4, core: 2. Of those that a mesh axis runs over, the one named last changes fastest.
Arguments:
- queue_latents: bfloat16 [64, 384, 3072], P('queue')
- fresh_noise: bfloat16 [2, 384, 3072], replicated, may hold values from -6 to 6
- levels: int32 [64], P('queue'), may hold values from 0 to 49, as said below
- window_start: int32 [64], P('queue'), may hold values from 0 to 61, as said below
- modulation: float32 [50, 3, 3072], replicated, may hold values from -3 to 3
- w_qkv: bfloat16 [3072, 3, 1536], P(None, None, 'tensor')
- qk_gain: float32 [2, 1536], P(None, 'tensor')
- w_out: bfloat16 [1536, 3072], P('tensor'), may hold values from -0.15625 to 0.15625
- sampler: float32 [50, 2], replicated, may hold values from 0.3 to 1
Outputs:
- advanced_queue: bfloat16 [64, 384, 3072], P('queue')
Inputs may be any that keep to these rules, and one draw needn't show every extreme that they name: `levels`: level indices grow along the queue: slot f has f * 50 // 64 or one more, at most 49. The window of slot f, window_start[f] to window_start[f] + 2, contains f; for even f it starts at f - 2 or f - 1, for odd f at f - 1 or f, in each case clipped to 0 to 61.
All inputs are finite; a program needn't handle non-finite values.
Results may differ from a plain program's by a relative error of at most 0.014.
Values may be sent and summed in bfloat16 or wider, within the bound.
A program may use at most 192 MiB of HBM per device.

v0:
```python
import jax
import jax.numpy as jnp
from jax import lax
from jax.sharding import PartitionSpec as P

HDIM = 64
WIN = 3
STEPS = 2


def with_halo(value, sides, width):
    for axis, dim in sides:
        devices, length = (lax.axis_size(axis), value.shape[dim])
        up = [(i, (i + 1) % devices) for i in range(devices - 1)]
        down = [(j, i) for i, j in up]
        last = lax.slice_in_dim(value, length - width, length, axis=dim)
        initial = lax.slice_in_dim(value, 0, width, axis=dim)
        before = lax.ppermute(last, axis, up)
        after = lax.ppermute(initial, axis, down)
        value = jnp.concatenate([before, value, after], axis=dim)
    return value


def from_behind(value, axis, steps):
    count = lax.axis_size(axis)
    initial, last = (max(0, -steps), min(count, count - steps))
    return lax.ppermute(value, axis, [(source, source + steps) for source in range(initial, last)])


def layer_norm(values, eps_value):
    mean = jnp.mean(values, axis=-1, keepdims=True)
    centered = values - mean
    var = jnp.mean(centered * centered, axis=-1, keepdims=True)
    return centered * lax.rsqrt(var + eps_value)


def modulated(rows_x, row_mod, width):
    values = rows_x.astype(jnp.float32)
    normed = (
        layer_norm(values, 1e-06) * (1.0 + row_mod[..., width : 2 * width]) + row_mod[..., :width]
    )
    return normed.astype(jnp.bfloat16)


def updated(rows_x, branch, row_mod, row_coef, width):
    values = rows_x.astype(jnp.float32)
    noise_pred = values + row_mod[..., 2 * width :] * branch
    return (row_coef[..., 0:1] * values + row_coef[..., 1:2] * noise_pred).astype(jnp.bfloat16)


def attention(qkv, qk_gain, window_start, frames_dev, frame_len):
    local_width = qk_gain.shape[1]
    heads_local = local_width // HDIM
    qkv = qkv.reshape(frames_dev, frame_len, 3, heads_local, HDIM)
    query = (layer_norm(qkv[:, :, 0], 1e-06) * qk_gain[0].reshape(heads_local, HDIM)).astype(
        jnp.bfloat16
    )
    keys = (layer_norm(qkv[:, :, 1], 1e-06) * qk_gain[1].reshape(heads_local, HDIM)).astype(
        jnp.bfloat16
    )
    values = qkv[:, :, 2].astype(jnp.bfloat16)
    packed = jnp.stack(
        [
            keys.reshape(frames_dev, frame_len, local_width),
            values.reshape(frames_dev, frame_len, local_width),
        ],
        axis=2,
    )
    packed = packed.reshape(frames_dev, frame_len, 2 * local_width)
    padded = with_halo(packed, (("queue", 0),), frames_dev)
    first_slot = lax.axis_index("queue") * frames_dev
    outputs = []
    for frame in range(frames_dev):
        offset = window_start[frame] - first_slot + frames_dev
        window = lax.dynamic_slice_in_dim(padded, offset, WIN, 0).reshape(
            WIN * frame_len, 2, heads_local, HDIM
        )
        scores = jnp.einsum(
            "qhd,khd->hqk", query[frame], window[:, 0], preferred_element_type=jnp.float32
        ) / jnp.sqrt(jnp.float32(HDIM))
        top = jnp.max(scores, axis=-1, keepdims=True)
        expo = jnp.exp(scores - top)
        weights = (expo / jnp.sum(expo, axis=-1, keepdims=True)).astype(jnp.bfloat16)
        out = jnp.einsum("hqk,khd->qhd", weights, window[:, 1], preferred_element_type=jnp.float32)
        outputs.append(out.astype(jnp.bfloat16).reshape(frame_len, local_width))
    return jnp.concatenate(outputs, axis=0)


def body(
    queue_latents, fresh_noise, levels, window_start, modulation, w_qkv, qk_gain, w_out, sampler
):
    frames_dev, frame_len, width = queue_latents.shape
    level_count = modulation.shape[0]
    queue_size = lax.axis_size("queue")
    queue_index = lax.axis_index("queue")
    total_rows = frames_dev * frame_len
    level_hot = (levels[:, None] == jnp.arange(level_count, dtype=jnp.int32)[None, :]).astype(
        jnp.float32
    )
    frame_mod = jnp.dot(
        level_hot, modulation.reshape(level_count, 3 * width), precision=lax.Precision.HIGHEST
    )
    frame_coef = jnp.dot(level_hot, sampler, precision=lax.Precision.HIGHEST)
    w_flat = w_qkv.reshape(width, 3 * w_qkv.shape[2])
    slot_mod = frame_mod[:, None, :]
    slot_coef = frame_coef[:, None, :]
    state = queue_latents
    for step in range(STEPS):
        hidden = modulated(state, slot_mod, width).reshape(total_rows, width)
        qkv = jnp.dot(hidden, w_flat, preferred_element_type=jnp.float32)
        attn = attention(qkv, qk_gain, window_start, frames_dev, frame_len)
        partial_out = jnp.dot(attn, w_out, preferred_element_type=jnp.float32)
        branch = (
            lax.psum(partial_out.astype(jnp.bfloat16), "tensor")
            .astype(jnp.float32)
            .reshape(frames_dev, frame_len, width)
        )
        new = updated(state, branch, slot_mod, slot_coef, width)
        moved = from_behind(new[0], "queue", -1)
        moved = jnp.where(queue_index == queue_size - 1, fresh_noise[step], moved)
        state = jnp.concatenate([new[1:], moved[None]], axis=0)
    return state


def solution(mesh):
    in_specs = (
        P("queue", None, None),
        P(),
        P("queue"),
        P("queue"),
        P(),
        P(None, None, "tensor"),
        P(None, "tensor"),
        P("tensor", None),
        P(),
    )
    out_specs = P("queue", None, None)
    return jax.shard_map(body, mesh=mesh, in_specs=in_specs, out_specs=out_specs, check_vma=False)
```

profile of v0, /device:TPU:102, one launch (start us, length us, event | category | flops | bytes accessed | tf_op | source)
XLA Modules:
  0.0 577.3 jit_solution(10760126688105388462)
XLA Ops:
  6.5 3.0 copy.11
  9.5 0.5 pad.18
  10.1 1.2 copy.27
  11.3 0.8 convolution_bitcast_fusion
  12.1 0.6 slice_bitcast_fusion.59
  12.7 10.3 %copy.12 = bf16[3072,3,384]{0,2,1:T(8,128)(2,1)} copy(bf16[3072,3,384]{2,0,1:T(8,128)(2,1)} %param.14) | data formatting | bytes 14155776 | tf_op args[5]
  23.0 3.2 convert_reduce_fusion.1
  26.2 3.9 fusion.12
  30.1 9.8 %fusion.43 = f32[2,384,3,6,64]{1,4,3,2,0:T(8,128)S(1)} fusion(bf16[3,6,64,3072,1]{3,2,1,0,4:T(8,128)(2,1)S(1)} %bitcast.249, bf16[2,384,3072]{2,1,0:T(8,128)(2,1)} %param.9, f32[2,3072]{1,0:T(2,128)S(1)} %get-tuple-element.27, f32[2,3072]{1,0:T(2,128)S(1)} %get-tuple-element.28, f32[2,384]{1,0:T(2,128)S(1)} %add_rsqrt_fusion.5, ...), kind=kOutput, calls=%fused_computation.58 | convolution fusion | flops 5449973760 | bytes 15390720 | tf_op jit(solution)/shard_map/dot_general | solution.py:110
  40.3 1.4 multiply_reduce_fusion.5
  42.4 2.0 collective-permute-start
  44.4 4.1 collective-permute-start.1
  48.5 0.7 fusion.102
  50.6 0.7 add_rsqrt_fusion.2
  51.3 2.3 multiply_convert_fusion.1
  53.6 18.5 %collective-permute-done = bf16[2,384,768]{1,2,0:T(8,128)(2,1)} collective-permute-done((bf16[2,384,768]{1,2,0:T(8,128)(2,1)S(1)}, bf16[2,384,768]{1,2,0:T(8,128)(2,1)}, u32[]{:S(2)}, u32[]{:S(2)}) %collective-permute-start) | collective-permute-done | bytes 1179680 | tf_op jit(solution)/shard_map/ppermute | solution.py:18
  72.1 6.1 %collective-permute-done.1 = bf16[2,384,768]{1,2,0:T(8,128)(2,1)} collective-permute-done((bf16[2,384,768]{1,2,0:T(8,128)(2,1)S(1)}, bf16[2,384,768]{1,2,0:T(8,128)(2,1)}, u32[]{:S(2)}, u32[]{:S(2)}) %collective-permute-start.1) | collective-permute-done | bytes 1179680 | tf_op jit(solution)/shard_map/ppermute | solution.py:19
  78.2 1.9 pad_maximum_fusion.2
  80.1 1.6 constant_dynamic-slice_fusion.3
  81.7 2.9 copy.16
  84.7 5.4 reshape.282
  90.1 4.5 copy.17
  94.5 5.4 reshape.284
  99.9 8.1 %fusion.104 = (f32[6,384]{1,0:T(8,128)S(1)}, f32[6,384,1152]{2,1,0:T(8,128)}) fusion(bf16[1152,2,6,64]{0,3,2,1:T(8,128)(2,1)} %reshape.282, bf16[2,384,6,64]{1,3,2,0:T(8,128)(2,1)S(1)} %copy-done.7), kind=kOutput, calls=%fused_computation.176 | convolution fusion | flops 347702400 | bytes 11805696 | tf_op jit(solution)/shard_map/sub | solution.py:82
  107.9 8.2 %fusion.103 = (f32[6,384]{1,0:T(8,128)S(1)}, f32[6,384,1152]{2,1,0:T(8,128)}) fusion(bf16[1152,2,6,64]{0,3,2,1:T(8,128)(2,1)} %reshape.284, bf16[2,384,6,64]{1,3,2,0:T(8,128)(2,1)S(1)} %copy-done.7), kind=kOutput, calls=%fused_computation.175 | convolution fusion | flops 347702400 | bytes 11805696 | tf_op jit(solution)/shard_map/sub | solution.py:82
  116.2 6.3 %fusion.61 = bf16[6,64,384]{2,1,0:T(8,128)(2,1)S(1)} fusion(f32[6,384,1152]{2,1,0:T(8,128)} %get-tuple-element.34, f32[6,384]{1,0:T(8,128)S(1)} %get-tuple-element.33, bf16[1152,2,6,64]{0,3,2,1:T(8,128)(2,1)} %reshape.282), kind=kOutput, calls=%fused_computation.82 | convolution fusion | flops 345194496 | bytes 11805696 | tf_op jit(solution)/shard_map/hqk,khd->qhd/dot_general | solution.py:84
  122.5 1.5 copy-done.18
  124.0 2.1 fusion.60
  126.2 4.3 convolution_convert_fusion.1
  130.5 11.6 %all-reduce.5.cloned.1.call-start = ((), (), s32[]{:S(2)}) async-start(), calls=%async_computation.1 | async-start | bytes 9437184 | tf_op jit(solution)/shard_map/psum | solution.py:114
  142.5 90.5 %all-reduce.3.cloned.1.call-done = bf16[2,384,3072]{2,1,0:T(8,128)(2,1)} async-done(((bf16[2,384,3072]{2,1,0:T(8,128)(2,1)}), bf16[2,384,3072]{2,1,0:T(8,128)(2,1)}) %all-reduce.3.cloned.1.call-update) | async-done | bytes 4718608 | tf_op jit(solution)/shard_map/psum | solution.py:114
  233.0 6.2 %fusion.17 = bf16[2,384,3072]{2,1,0:T(8,128)(2,1)S(1)} fusion(bf16[2,384,3072]{2,1,0:T(8,128)(2,1)} %param.9, bf16[2,384,3072]{2,1,0:T(8,128)(2,1)} %all-reduce.3.cloned.1.call-done, f32[2,3072]{1,0:T(2,128)S(1)} %copy-done.9, f32[2]{0:T(128)S(1)} %get-tuple-element.14, f32[2]{0:T(128)S(1)} %get-tuple-element.13), kind=kLoop, calls=%fused_computation.34 | loop fusion | flops 18874368 | bytes 14180368 | tf_op jit(solution)/shard_map/convert_element_type | solution.py:48
  239.2 2.5 fusion.100
  241.7 2.7 collective-permute-start.2
  244.4 57.2 %collective-permute-done.2 = bf16[384,3072]{1,0:T(8,128)(2,1)} collective-permute-done((bf16[384,3072]{1,0:T(8,128)(2,1)}, bf16[384,3072]{1,0:T(8,128)(2,1)}, u32[]{:S(2)}, u32[]{:S(2)}) %collective-permute-start.2) | collective-permute-done | bytes 2359328 | tf_op jit(solution)/shard_map/ppermute | solution.py:27
  301.6 2.8 fusion.57
  304.4 0.7 convert_reduce_fusion
  305.1 1.4 fusion.8
  306.5 0.7 slice-done.1
  307.2 6.1 %fusion.46 = f32[2,384,3,6,64]{1,4,3,2,0:T(8,128)S(1)} fusion(bf16[3,6,64,3072,1]{3,2,1,0,4:T(8,128)(2,1)S(1)} %bitcast.252, f32[2,384]{1,0:T(2,128)S(1)} %add_rsqrt_fusion.4, f32[2,384]{1,0:T(2,128)S(1)} %broadcast_multiply_fusion.4, f32[2,3072]{1,0:T(2,128)S(1)} %copy-done.11, f32[2,3072]{1,0:T(2,128)S(1)} %copy-done.13, ...), kind=kOutput, calls=%fused_computation.60 | convolution fusion | flops 5457051648 | bytes 15390720 | tf_op jit(solution)/shard_map/dot_general | solution.py:110
  313.7 0.3 multiply_reduce_fusion.4
  314.6 1.9 collective-permute-start.3
  316.5 3.9 collective-permute-start.4
  320.7 23.1 %collective-permute-done.3 = bf16[2,384,768]{1,2,0:T(8,128)(2,1)S(1)} collective-permute-done((bf16[2,384,768]{1,2,0:T(8,128)(2,1)S(1)}, bf16[2,384,768]{1,2,0:T(8,128)(2,1)S(1)}, u32[]{:S(2)}, u32[]{:S(2)}) %collective-permute-start.3) | collective-permute-done | bytes 1179680 | tf_op jit(solution)/shard_map/ppermute | solution.py:18
  343.8 6.1 %collective-permute-done.4 = bf16[2,384,768]{1,2,0:T(8,128)(2,1)S(1)} collective-permute-done((bf16[2,384,768]{1,2,0:T(8,128)(2,1)S(1)}, bf16[2,384,768]{1,2,0:T(8,128)(2,1)S(1)}, u32[]{:S(2)}, u32[]{:S(2)}) %collective-permute-start.4) | collective-permute-done | bytes 1179680 | tf_op jit(solution)/shard_map/ppermute | solution.py:19
  350.0 0.5 pad_maximum_fusion.3
  350.5 1.7 constant_dynamic-slice_fusion.1
  352.1 2.9 copy.21
  355.0 5.3 reshape.289
  360.4 4.4 copy.23
  364.8 5.5 reshape.291
  370.3 8.1 %fusion.106 = (f32[6,384]{1,0:T(8,128)S(1)}, f32[6,384,1152]{2,1,0:T(8,128)}) fusion(bf16[1152,2,6,64]{0,3,2,1:T(8,128)(2,1)} %reshape.289, bf16[2,384,6,64]{1,3,2,0:T(8,128)(2,1)S(1)} %multiply_convert_fusion), kind=kOutput, calls=%fused_computation.178 | convolution fusion | flops 347702400 | bytes 11805696 | tf_op jit(solution)/shard_map/sub | solution.py:82
  378.4 8.2 %fusion.105 = (f32[6,384]{1,0:T(8,128)S(1)}, f32[6,384,1152]{2,1,0:T(8,128)}) fusion(bf16[1152,2,6,64]{0,3,2,1:T(8,128)(2,1)} %reshape.291, bf16[2,384,6,64]{1,3,2,0:T(8,128)(2,1)S(1)} %multiply_convert_fusion), kind=kOutput, calls=%fused_computation.177 | convolution fusion | flops 347702400 | bytes 11805696 | tf_op jit(solution)/shard_map/sub | solution.py:82
  386.6 6.3 %fusion.59 = bf16[6,64,384]{2,1,0:T(8,128)(2,1)S(1)} fusion(f32[6,384,1152]{2,1,0:T(8,128)} %get-tuple-element.38, f32[6,384]{1,0:T(8,128)S(1)} %get-tuple-element.37, bf16[1152,2,6,64]{0,3,2,1:T(8,128)(2,1)} %reshape.289), kind=kOutput, calls=%fused_computation.80 | convolution fusion | flops 345194496 | bytes 11805696 | tf_op jit(solution)/shard_map/hqk,khd->qhd/dot_general | solution.py:84
  392.9 1.5 copy-done.19
  394.4 2.1 fusion.58
  396.6 4.3 convolution_convert_fusion
  400.9 99.9 %all-reduce.5.cloned.1.call-done = bf16[2,384,3072]{2,1,0:T(8,128)(2,1)} async-done(((bf16[2,384,3072]{2,1,0:T(8,128)(2,1)}), bf16[2,384,3072]{2,1,0:T(8,128)(2,1)}) %all-reduce.5.cloned.1.call-update) | async-done | bytes 4718608 | tf_op jit(solution)/shard_map/psum | solution.py:114
  500.8 4.9 fusion.20
  505.7 0.3 fusion.99
  506.1 2.7 collective-permute-start.5
  508.8 56.9 %collective-permute-done.5 = bf16[384,3072]{1,0:T(8,128)(2,1)S(1)} collective-permute-done((bf16[384,3072]{1,0:T(8,128)(2,1)S(1)}, bf16[384,3072]{1,0:T(8,128)(2,1)S(1)}, u32[]{:S(2)}, u32[]{:S(2)}) %collective-permute-start.5) | collective-permute-done | bytes 2359328 | tf_op jit(solution)/shard_map/ppermute | solution.py:27
  565.6 1.9 fusion.56
  567.5 2.6 pad_maximum_fusion.1
  (73 shorter events, 2.5 us)
Async XLA Ops:
  6.5 119.6 %copy-start = (bf16[384,3072]{1,0:T(8,128)(2,1)S(1)}, bf16[384,3072]{1,0:T(8,128)(2,1)}, u32[]{:S(2)}) copy-start(bf16[384,3072]{1,0:T(8,128)(2,1)} %param.16) | copy-start | bytes 7077892
  6.5 226.5 %all-reduce.3.cloned.1.call-start = ((), (), s32[]{:S(2)}) async-start(), calls=%async_computation | async-start | bytes 9437184 | tf_op jit(solution)/shard_map/psum | solution.py:114
  10.1 1.2 copy-start.16
  12.7 17.4 %copy-start.10 = (f32[2,3072]{1,0:T(2,128)}, f32[2,3072]{1,0:T(2,128)S(1)}, u32[]{:S(2)}) copy-start(f32[2,3072]{1,0:T(2,128)S(1)} %get-tuple-element.27) | copy-start | bytes 73732
  12.7 17.5 %copy-start.12 = (f32[2,3072]{1,0:T(2,128)}, f32[2,3072]{1,0:T(2,128)S(1)}, u32[]{:S(2)}) copy-start(f32[2,3072]{1,0:T(2,128)S(1)} %get-tuple-element.28) | copy-start | bytes 73732
  23.0 7.2 %copy-start.4 = (bf16[3072,3,384]{0,2,1:T(8,128)(2,1)S(1)}, bf16[3072,3,384]{0,2,1:T(8,128)(2,1)}, u32[]{:S(2)}) copy-start(bf16[3072,3,384]{0,2,1:T(8,128)(2,1)} %copy.12) | copy-start | bytes 21233668
  40.0 1.8 copy-start.3
  40.0 1.8 copy-start.14
  40.3 1.5 copy-start.8
  42.0 6.5 %copy-start.15 = (s32[2]{0:T(128)S(1)}, s32[2]{0:T(128)}, u32[]{:S(2)}) copy-start(s32[2]{0:T(128)} %param.12) | copy-start | bytes 28
  42.4 29.7 %collective-permute-start = (bf16[2,384,768]{1,2,0:T(8,128)(2,1)S(1)}, bf16[2,384,768]{1,2,0:T(8,128)(2,1)}, u32[]{:S(2)}, u32[]{:S(2)}) collective-permute-start(bf16[2,384,768]{1,2,0:T(8,128)(2,1)S(1)} %bitcast.253), channel_id=1, source_target_pairs={{0,4},{4,8},{8,12},{12,16},{16,20},{20,24},{24,28},{28,32},{32,36}... | collective-permute-start | bytes 3538952 | tf_op jit(solution)/shard_map/ppermute | solution.py:18
  44.4 33.8 %collective-permute-start.1 = (bf16[2,384,768]{1,2,0:T(8,128)(2,1)S(1)}, bf16[2,384,768]{1,2,0:T(8,128)(2,1)}, u32[]{:S(2)}, u32[]{:S(2)}) collective-permute-start(bf16[2,384,768]{1,2,0:T(8,128)(2,1)S(1)} %bitcast.254), channel_id=1, source_target_pairs={{4,0},{8,4},{12,8},{16,12},{20,16},{24,20},{28,24},{32,28},{36,32}... | collective-permute-start | bytes 3538952 | tf_op jit(solution)/shard_map/ppermute | solution.py:19
  90.1 9.8 %copy-start.7 = (bf16[2,384,6,64]{1,3,2,0:T(8,128)(2,1)S(1)}, bf16[2,384,6,64]{1,3,2,0:T(8,128)(2,1)}, u32[]{:S(2)}) copy-start(bf16[2,384,6,64]{1,3,2,0:T(8,128)(2,1)} %multiply_convert_fusion.1) | copy-start | bytes 1769476
  116.2 6.3 %copy-start.5 = (bf16[1152,2,6,64]{0,3,2,1:T(8,128)(2,1)S(1)}, bf16[1152,2,6,64]{0,3,2,1:T(8,128)(2,1)}, u32[]{:S(2)}) copy-start(bf16[1152,2,6,64]{0,3,2,1:T(8,128)(2,1)} %reshape.284) | copy-start | bytes 5308420
  116.2 7.8 %copy-start.18 = (f32[6,384,1152]{2,1,0:T(8,128)S(1)}, f32[6,384,1152]{2,1,0:T(8,128)}, u32[]{:S(2)}) copy-start(f32[6,384,1152]{2,1,0:T(8,128)} %get-tuple-element.32) | copy-start | bytes 31850500
  130.5 11.6 %copy-start.17 = (f32[50,2]{0,1:T(2,128)S(1)}, f32[50,2]{0,1:T(2,128)}, u32[]{:S(2)}) copy-start(f32[50,2]{0,1:T(2,128)} %param.17) | copy-start | bytes 1204
  130.5 102.5 %copy-start.9 = (f32[2,3072]{1,0:T(2,128)S(1)}, f32[2,3072]{1,0:T(2,128)}, u32[]{:S(2)}) copy-start(f32[2,3072]{1,0:T(2,128)} %get-tuple-element.26) | copy-start | bytes 73732
  130.5 370.3 %all-reduce.5.cloned.1.call-start = ((), (), s32[]{:S(2)}) async-start(), calls=%async_computation.1 | async-start | bytes 9437184 | tf_op jit(solution)/shard_map/psum | solution.py:114
  241.7 59.8 %collective-permute-start.2 = (bf16[384,3072]{1,0:T(8,128)(2,1)}, bf16[384,3072]{1,0:T(8,128)(2,1)}, u32[]{:S(2)}, u32[]{:S(2)}) collective-permute-start(bf16[384,3072]{1,0:T(8,128)(2,1)} %get-tuple-element.18), channel_id=1, source_target_pairs={{4,0},{8,4},{12,8},{16,12},{20,16},{24,20},{28,24},{32,28},{36,32}... | collective-permute-start | bytes 7077896 | tf_op jit(solution)/shard_map/ppermute | solution.py:27
  244.4 60.0 %copy-start.2 = (bf16[1,384,3072]{2,1,0:T(8,128)(2,1)S(1)}, bf16[1,384,3072]{2,1,0:T(8,128)(2,1)}, u32[]{:S(2)}) copy-start(bf16[1,384,3072]{2,1,0:T(8,128)(2,1)} %get-tuple-element.17) | copy-start | bytes 7077892
  301.6 4.9 slice-start
  304.4 2.1 copy-start.1
  304.4 2.9 slice-start.1
  305.1 2.2 copy-start.11
  305.1 2.2 copy-start.13
  314.6 29.2 %collective-permute-start.3 = (bf16[2,384,768]{1,2,0:T(8,128)(2,1)S(1)}, bf16[2,384,768]{1,2,0:T(8,128)(2,1)S(1)}, u32[]{:S(2)}, u32[]{:S(2)}) collective-permute-start(bf16[2,384,768]{1,2,0:T(8,128)(2,1)S(1)} %bitcast.256), channel_id=1, source_target_pairs={{0,4},{4,8},{8,12},{12,16},{16,20},{20,24},{24,28},{28,32},{32,36}... | collective-permute-start | bytes 3538952 | tf_op jit(solution)/shard_map/ppermute | solution.py:18
  316.5 33.4 %collective-permute-start.4 = (bf16[2,384,768]{1,2,0:T(8,128)(2,1)S(1)}, bf16[2,384,768]{1,2,0:T(8,128)(2,1)S(1)}, u32[]{:S(2)}, u32[]{:S(2)}) collective-permute-start(bf16[2,384,768]{1,2,0:T(8,128)(2,1)S(1)} %bitcast.257), channel_id=1, source_target_pairs={{4,0},{8,4},{12,8},{16,12},{20,16},{24,20},{28,24},{32,28},{36,32}... | collective-permute-start | bytes 3538952 | tf_op jit(solution)/shard_map/ppermute | solution.py:19
  386.6 6.3 %copy-start.6 = (bf16[1152,2,6,64]{0,3,2,1:T(8,128)(2,1)S(1)}, bf16[1152,2,6,64]{0,3,2,1:T(8,128)(2,1)}, u32[]{:S(2)}) copy-start(bf16[1152,2,6,64]{0,3,2,1:T(8,128)(2,1)} %reshape.291) | copy-start | bytes 5308420
  386.6 7.8 %copy-start.19 = (f32[6,384,1152]{2,1,0:T(8,128)S(1)}, f32[6,384,1152]{2,1,0:T(8,128)}, u32[]{:S(2)}) copy-start(f32[6,384,1152]{2,1,0:T(8,128)} %get-tuple-element.36) | copy-start | bytes 31850500
  506.1 59.5 %collective-permute-start.5 = (bf16[384,3072]{1,0:T(8,128)(2,1)S(1)}, bf16[384,3072]{1,0:T(8,128)(2,1)S(1)}, u32[]{:S(2)}, u32[]{:S(2)}) collective-permute-start(bf16[384,3072]{1,0:T(8,128)(2,1)S(1)} %get-tuple-element.16), channel_id=1, source_target_pairs={{4,0},{8,4},{12,8},{16,12},{20,16},{24,20},{28,24},{32,28},{36,32}... | collective-permute-start | bytes 7077896 | tf_op jit(solution)/shard_map/ppermute | solution.py:27
Sparse Core Ops, SparseCore 0:
  130.6 102.3 all-reduce.2
  401.0 99.7 all-reduce.4
where the time goes:
time: 587 us; the launch traced here: 577 us
  waiting for transfers between devices  358 us (61%)
  matrix products  75.1 us (13%)
  local copies, waits for them, and re-layouts  62.7 us (11%)
  other arithmetic  36.7 us (6%)
  starting transfers between devices  28.9 us (5%)
  between operations  15.6 us (3%)
    psum x2, waiting for transfers between devices, body(): lax.psum(partial_out.astype(jnp.bfloat16), 'tensor').astype(jnp.float32)  190 us
    ppermute x2, waiting for transfers between devices, from_behind(): lax.ppermute(value, axis, [(source, source + steps) for source in range(i...  114 us
    ppermute x2, waiting for transfers between devices, with_halo(): before = lax.ppermute(last, axis, up)  41.6 us
    sub x4, matrix products, attention(): expo = jnp.exp(scores - top)  32.6 us
    reshape x4, local copies, waits for them, and re-layouts, attention(): lax.dynamic_slice_in_dim(padded, offset, WIN, 0)  21.6 us
    unnamed x48, local copies, waits for them, and re-layouts  18.9 us
    dynamic_slice x6, local copies, waits for them, and re-layouts, attention(): lax.dynamic_slice_in_dim(padded, offset, WIN, 0)  18 us
    dot_general x4, matrix products, attention(): jnp.einsum('hqk,khd->qhd', weights, window[:, 1], preferred_element_type=...  17 us
  transfers between devices with their start and end apart: 8, of which 8 were waited for; matrix products, arithmetic and copies ran while one was open for 1% of the time, Pallas kernels for 0%

commit v1 on v0

v1 whole, which is shorter than its diff:
```python
import functools

import jax
import jax.numpy as jnp
from jax import lax
from jax.experimental import pallas as pl
from jax.experimental.pallas import tpu as pltpu
from jax.sharding import PartitionSpec as P

MESH = pl.DeviceIdType.MESH
BF16 = jnp.bfloat16
F32 = jnp.float32
STEPS = 2
WIN = 3
EPS = 1e-6

SEM = {}


def slots(name, count):
    SEM[name] = sum(n for _, n in SEM.values()), count


slots("halo_up", 6)
slots("halo_down", 6)
slots("halo_wrap", 3)
slots("attn_core", 6)
slots("attn_y", 6)
slots("attn_fwd", 6)
slots("wout_core", 1)
slots("wout_y", 4)
slots("wout_x", 4)
slots("gather", 6)
slots("shift", 4)
slots("out_y", 4)
slots("out_core", 4)
slots("out_fwd", 4)
slots("meta", 1)
N_SEM = sum(n for _, n in SEM.values())


def kernel(
    frame, width, heads_width,
    x_in, fresh, levels, window_start, mod_in, w_in, gain, wout_in, sampler,
    out,
    x0, x1, h, wkv, wq, wfull, q, attn0, attn1, kv00, kv01, kv02, kv10, kv11, kv12,
    chosen, xs, mod, slot0, slot1, lsem, ssem, rsem,
):
    rows = 2 * frame
    half = width // 2
    quarter = width // 4
    pairs = heads_width // 128
    qi = lax.axis_index("queue")
    ti = lax.axis_index("tensor")
    n_queue = lax.axis_size("queue")
    core = lax.rem(ti, 2)
    chip = lax.div(ti, 2)
    t_core = chip * 2 + (1 - core)
    t_y = lax.rem(ti + 2, 4)
    t_far = 3 - ti
    up = lax.rem(qi + 1, n_queue)
    down = lax.rem(qi + n_queue - 1, n_queue)
    across = lax.rem(qi + n_queue // 2, n_queue)
    plane = lax.div(qi, 16) * 16
    x_up = plane + lax.rem(qi + 4, 16)
    x_down = plane + lax.rem(qi + 12, 16)
    x_pos = lax.div(lax.rem(qi, 16), 4)
    first = qi == 0
    final = qi == n_queue - 1

    def rcopy(name, index, src, dst, device):
        slot = SEM[name][0] + index
        return pltpu.make_async_remote_copy(
            src_ref=src, dst_ref=dst, send_sem=ssem.at[slot], recv_sem=rsem.at[slot],
            device_id=device, device_id_type=MESH,
        )

    def landed(name, index, ref):
        rcopy(name, index, ref, ref, (qi, t_core)).wait_recv()

    def local(index, src, dst):
        return pltpu.make_async_copy(src, dst, lsem.at[index])

    def at_lane(start, size):
        return pl.ds(pl.multiple_of(start, 128), size)

    def at_row(start, size):
        return pl.ds(pl.multiple_of(start, 16), size)

    load_x = local(0, x_in, x0)
    load_mod = local(1, mod_in, mod)
    load_x.start()
    load_mod.start()
    load_w = []
    for p in range(pairs):
        for j in (1, 2):
            load_w.append(
                local(1 + 2 * p + j, w_in.at[j, :, p * 128 : (p + 1) * 128],
                      wkv.at[p, :, (j - 1) * 128 : j * 128])
            )
    load_w.append(local(8, w_in.at[0], wq))
    for load in load_w:
        load.start()
    my_half = at_lane(core * half, half)
    other_half = at_lane((1 - core) * half, half)
    load_wout = local(9, wout_in.at[:, my_half], wfull.at[at_row(ti * heads_width, heads_width)])
    load_wout.start()

    barrier = pltpu.get_barrier_semaphore()
    partners = [
        (up, ti), (down, ti), (qi, t_core), (qi, t_y),
        (across, t_y), (across, t_far), (x_up, ti), (x_down, ti),
    ]
    for device in partners:
        pl.semaphore_signal(barrier, inc=1, device_id=device, device_id_type=MESH)
    pl.semaphore_wait(barrier, len(partners))

    sends = []

    def send(name, index, src, dst, device):
        copy = rcopy(name, index, src, dst, device)
        copy.start()
        sends.append((None, copy))
        return copy

    def send_if(cond, name, index, src, dst, device):
        copy = rcopy(name, index, src, dst, device)

        @pl.when(cond)
        def _():
            copy.start()

        sends.append((cond, copy))

    piece = heads_width // 4

    def my_piece(k):
        return lax.rem(x_pos + k, 4) * piece

    def wout_rows(t, k):
        return wfull.at[at_row(t * heads_width + my_piece(k), piece)]

    def wout_src(k, columns):
        return wout_in.at[at_row(my_piece(k), piece), columns]

    send("wout_y", 0, wout_src(0, my_half), wout_rows(ti, 0), (across, t_y))
    send("wout_y", 1, wout_src(0, other_half), wout_rows(ti, 0), (across, t_far))
    send("wout_core", 0, wout_in.at[:, other_half],
         wfull.at[at_row(ti * heads_width, heads_width)], (qi, t_core))
    send("wout_y", 2, wout_src(2, my_half), wout_rows(ti, 2), (across, t_y))
    send("wout_y", 3, wout_src(2, other_half), wout_rows(ti, 2), (across, t_far))

    def forward_wout():
        for i, t in enumerate((t_y, t_far)):
            landed("wout_y", i, wout_rows(t, 0))
            send("wout_x", i, wout_rows(t, 0), wout_rows(t, 0), (x_up, ti))
            send("wout_x", 2 + i, wout_rows(t, 0), wout_rows(t, 0), (x_down, ti))

    def finish_wout():
        load_wout.wait()
        landed("wout_core", 0, wfull.at[at_row(t_core * heads_width, heads_width)])
        for i, t in enumerate((t_y, t_far)):
            landed("wout_y", 2 + i, wout_rows(t, 2))
            landed("wout_x", i, wout_rows(t, 3))
            landed("wout_x", 2 + i, wout_rows(t, 1))

    row_head = lax.broadcasted_iota(jnp.int32, (128, 128), 0) >> 6
    col_head = lax.broadcasted_iota(jnp.int32, (128, 128), 1) >> 6
    head_mean = jnp.where(row_head == col_head, 1.0 / 64.0, 0.0).astype(BF16)

    def head_norm(values, gain_row):
        high = values.astype(BF16)
        low = (values - high.astype(F32)).astype(BF16)
        mean = jnp.dot(high, head_mean, preferred_element_type=F32)
        mean = mean + jnp.dot(low, head_mean, preferred_element_type=F32)
        centered = values - mean
        var = jnp.dot((centered * centered).astype(BF16), head_mean, preferred_element_type=F32)
        return (centered * lax.rsqrt(var + EPS) * gain_row).astype(BF16)

    for f in range(2):
        slot0[f, 3:4, :] = jnp.full((1, width), sampler[0, levels[f]], F32)
        slot0[f, 4:5, :] = jnp.full((1, width), sampler[1, levels[f]], F32)
        slot0[f, 5:8, :] = jnp.full((3, width), window_start[f].astype(F32), F32)
    load_mod.wait()
    for f in range(2):
        for j in range(3):
            slot0[f, j : j + 1, :] = mod[j, pl.ds(levels[f], 1), :]
    send("meta", 0, slot0.at[1], slot1, (up, ti))

    def norm_rows(src, params):
        chunk = 16
        for f in range(2):
            param = params[f]

            @pl.loop(0, frame // chunk)
            def _(i):
                at = pl.ds(pl.multiple_of(f * frame + i * chunk, chunk), chunk)
                values = src[at, :].astype(F32)
                mean = jnp.mean(values, axis=-1, keepdims=True)
                centered = values - mean
                var = jnp.mean(centered * centered, axis=-1, keepdims=True)
                normed = centered * lax.rsqrt(var + EPS)
                h[at, :] = (
                    normed * (1.0 + param[1:2, :]) + param[0:1, :]
                ).astype(BF16)

    def project_kv(kv, p):
        @pl.loop(0, 2)
        def _(f):
            at = pl.ds(pl.multiple_of(f * frame, frame), frame)
            acc = jnp.dot(h[at, :], wkv[p], preferred_element_type=F32)
            kv[f + 2, :, 0:128] = head_norm(acc[:, :128], gain[1:2, p * 128 : (p + 1) * 128])
            kv[f + 2, :, 128:256] = acc[:, 128:].astype(BF16)

    def project_q():
        @pl.loop(0, 2)
        def _(f):
            at = pl.ds(pl.multiple_of(f * frame, frame), frame)
            acc = jnp.dot(h[at, :], wq[...], preferred_element_type=F32)
            for p in range(pairs):
                cols = slice(p * 128, (p + 1) * 128)
                q[at, cols] = head_norm(acc[:, cols], gain[0:1, cols]) * jnp.asarray(0.125, BF16)

    q_chunk = frame // 2
    first_head = lax.broadcasted_iota(jnp.int32, (q_chunk, 128), 1) < 64
    zeros = jnp.zeros((q_chunk, 128), BF16)
    ones = jnp.ones((WIN * frame, 128), BF16)

    def attend(kv, p, f, window, flag, attn):
        fixed, second, if_set, if_clear = window
        chosen[...] = jnp.where(
            flag, kv[if_set].astype(F32), kv[if_clear].astype(F32)
        ).astype(BF16)

        @pl.loop(0, 2)
        def _(i):
            at = pl.ds(pl.multiple_of(f * frame + i * q_chunk, 16), q_chunk)
            keys = jnp.concatenate(
                [kv[fixed, :, 0:128], kv[second, :, 0:128], chosen[:, 0:128]], axis=0
            )
            values = jnp.concatenate(
                [kv[fixed, :, 128:256], kv[second, :, 128:256], chosen[:, 128:256]], axis=0
            )
            values = jnp.concatenate([values, ones], axis=1)
            rows_q = q[at, p * 128 : (p + 1) * 128]
            both = jnp.concatenate(
                [jnp.where(first_head, rows_q, zeros), jnp.where(first_head, zeros, rows_q)], axis=0
            )
            scores = lax.dot_general(
                both, keys, (((1,), (1,)), ((), ())), preferred_element_type=F32
            )
            top = jnp.max(scores, axis=-1, keepdims=True)
            expo = jnp.exp(scores - top).astype(BF16)
            total = jnp.dot(expo, values, preferred_element_type=F32)
            mixed = total[:, :128] / total[:, 128:]
            attn[at, at_lane(ti * heads_width + p * 128, 128)] = jnp.where(
                first_head, mixed[:q_chunk], mixed[q_chunk:]
            ).astype(BF16)

    def attn_block(attn, t, p):
        return attn.at[:, at_lane(t * heads_width + p * 128, 128)]

    def share_attn(step, attn, p):
        mine = attn_block(attn, ti, p)
        send("attn_core", step * 3 + p, mine, mine, (qi, t_core))
        send("attn_y", step * 3 + p, mine, mine, (qi, t_y))

    def forward_attn(step, attn, p):
        block = attn_block(attn, t_y, p)
        landed("attn_y", step * 3 + p, block)
        send("attn_fwd", step * 3 + p, block, block, (qi, t_core))

    def finish_attn(step, attn):
        for p in range(pairs):
            landed("attn_core", step * 3 + p, attn_block(attn, t_core, p))
        for p in range(pairs):
            landed("attn_fwd", step * 3 + p, attn_block(attn, t_far, p))

    def update(values, branch, param, columns):
        values = values.astype(F32)
        noise_pred = values + param[2:3, columns] * branch
        return (param[3:4, columns] * values + param[4:5, columns] * noise_pred).astype(BF16)

    kv0 = (kv00, kv01, kv02)
    kv1 = (kv10, kv11, kv12)
    param0 = (slot0.at[0], slot0.at[1])
    param1 = (slot1, slot0.at[0])
    window0 = (
        (2, jnp.where(first, 4, 1), 3, 0),
        (3, jnp.where(final, 1, 4), 5, 2),
    )
    window1 = (
        (2, jnp.where(first, 0, 3), jnp.where(first, 1, 4), 1),
        (3, 2, 4, 1),
    )

    def starts_from(param, slot):
        start = jnp.concatenate([param[5:6, 0:128]] * 2, axis=1)
        return start >= slot.astype(F32)

    load_x.wait()
    norm_rows(x0, param0)
    for p in range(pairs):
        load_w[2 * p].wait()
        load_w[2 * p + 1].wait()
        project_kv(kv0[p], p)
        own = kv0[p].at[2:4]
        send_if(jnp.logical_not(final), "halo_up", p, own, kv0[p].at[0:2], (up, ti))
        send_if(jnp.logical_not(first), "halo_down", p, own, kv0[p].at[4:6], (down, ti))
    load_w[6].wait()
    project_q()
    for p in range(pairs):
        if p == 1:
            forward_wout()

        @pl.when(jnp.logical_not(first))
        def _():
            landed("halo_up", p, kv0[p].at[0:2])

        @pl.when(jnp.logical_not(final))
        def _():
            landed("halo_down", p, kv0[p].at[4:6])

        for f in range(2):
            attend(kv0[p], p, f, window0[f], starts_from(param0[f], 2 * qi - 1 + 2 * f), attn0)
        share_attn(0, attn0, p)
        if p > 0:
            forward_attn(0, attn0, p - 1)
    forward_attn(0, attn0, pairs - 1)
    finish_wout()
    finish_attn(0, attn0)

    n_cols = 256

    @pl.loop(0, half // n_cols)
    def _(n):
        columns = at_lane(core * half + n * n_cols, n_cols)
        weight = wfull[:, at_lane(n * n_cols, n_cols)]
        for f in range(2):
            at = slice(f * frame, (f + 1) * frame)
            branch = jnp.dot(attn0[at, :], weight, preferred_element_type=F32)
            x1[at, columns] = update(x0[at, columns], branch, param0[f], columns)
        rcopy("gather", n, x1.at[:, columns], x1.at[:, columns], (qi, t_core)).start()

    @pl.loop(0, half // n_cols)
    def _(n):
        theirs = at_lane((1 - core) * half + n * n_cols, n_cols)
        columns = at_lane(core * half + n * n_cols, n_cols)
        rcopy("gather", n, x1.at[:, columns], x1.at[:, theirs], (qi, t_core)).wait_send()
        landed("gather", n, x1.at[:, theirs])

    @pl.when(first)
    def _():
        entered = local(0, fresh.at[0], x1.at[0:frame])
        entered.start()
        entered.wait()

    landed("meta", 0, slot1)
    norm_rows(x1, param1)
    for p in range(pairs):
        project_kv(kv1[p], p)
        send("halo_up", 3 + p, kv1[p].at[3], kv1[p].at[1], (up, ti))
        send("halo_down", 3 + p, kv1[p].at[2], kv1[p].at[4], (down, ti))
        send_if(final, "halo_wrap", p, kv1[p].at[2], kv1[p].at[0], (up, ti))
    project_q()
    for p in range(pairs):
        landed("halo_up", 3 + p, kv1[p].at[1])
        landed("halo_down", 3 + p, kv1[p].at[4])

        @pl.when(first)
        def _():
            landed("halo_wrap", p, kv1[p].at[0])

        for f in range(2):
            attend(kv1[p], p, f, window1[f], starts_from(param1[f], 2 * qi - 1), attn1)
        share_attn(1, attn1, p)
        if p > 0:
            forward_attn(1, attn1, p - 1)
    forward_attn(1, attn1, pairs - 1)
    finish_attn(1, attn1)

    chunks = 4
    n_rows = rows // chunks
    my_quarter = core * half + chip * quarter
    y_quarter = core * half + (1 - chip) * quarter

    def out_part(j, start):
        return out.at[at_row(j * n_rows, n_rows), at_lane(start, quarter)]

    for j in range(chunks):
        f = j // 2
        at = slice(j * n_rows, (j + 1) * n_rows)

        @pl.loop(0, quarter // n_cols)
        def _(n):
            columns = at_lane(my_quarter + n * n_cols, n_cols)
            inner = at_lane(n * n_cols, n_cols)
            weight = wfull[:, at_lane(chip * quarter + n * n_cols, n_cols)]
            branch = jnp.dot(attn1[at, :], weight, preferred_element_type=F32)
            xs[at, inner] = update(x1[at, columns], branch, param1[f], columns)

        part = (xs.at[at], out_part(j, my_quarter), (down, ti))
        if f == 0:
            send("shift", j, *part)
        else:
            send_if(jnp.logical_not(first), "shift", j, *part)

    @pl.when(final)
    def _():
        last = local(0, fresh.at[1], out.at[frame:rows])
        last.start()
        last.wait()

    def guarded(f, action):
        if f == 0:
            action()
        else:
            pl.when(jnp.logical_not(final))(action)

    def spread(j):
        def action():
            part = out_part(j, my_quarter)
            landed("shift", j, part)
            rcopy("out_y", j, part, part, (qi, t_y)).start()
            rcopy("out_core", j, part, part, (qi, t_core)).start()

        guarded(j // 2, action)

    def pass_on(j):
        def action():
            part = out_part(j, y_quarter)
            landed("out_y", j, part)
            rcopy("out_fwd", j, part, part, (qi, t_core)).start()

        guarded(j // 2, action)

    for j in range(chunks):
        spread(j)
        if j > 0:
            pass_on(j - 1)
    pass_on(chunks - 1)

    core_quarter = (1 - core) * half + chip * quarter
    far_quarter = (1 - core) * half + (1 - chip) * quarter
    for j in range(chunks):

        def action():
            landed("out_core", j, out_part(j, core_quarter))
            landed("out_fwd", j, out_part(j, far_quarter))
            mine = out_part(j, my_quarter)
            rcopy("out_y", j, mine, mine, (qi, t_y)).wait_send()
            rcopy("out_core", j, mine, mine, (qi, t_core)).wait_send()
            passed = out_part(j, y_quarter)
            rcopy("out_fwd", j, passed, passed, (qi, t_core)).wait_send()

        guarded(j // 2, action)

    for cond, copy in sends:
        if cond is None:
            copy.wait_send()
        else:
            pl.when(cond)(copy.wait_send)


def body(
    queue_latents, fresh_noise, levels, window_start, modulation, w_qkv, qk_gain, w_out, sampler
):
    frames, frame, width = queue_latents.shape
    rows = frames * frame
    heads_width = w_out.shape[0]
    level_count = modulation.shape[0]
    any_space = pl.BlockSpec(memory_space=pl.ANY)
    smem = pl.BlockSpec(memory_space=pltpu.SMEM)
    vmem = pl.BlockSpec(memory_space=pltpu.VMEM)
    kv = pltpu.VMEM((6, frame, 256), BF16)
    result = pl.pallas_call(
        functools.partial(kernel, frame, width, heads_width),
        name="diagonal_steps",
        out_shape=jax.ShapeDtypeStruct((rows, width), BF16),
        in_specs=[any_space, any_space, smem, smem, any_space, any_space, vmem, any_space, smem],
        out_specs=any_space,
        scratch_shapes=[
            pltpu.VMEM((rows, width), BF16),
            pltpu.VMEM((rows, width), BF16),
            pltpu.VMEM((rows, width), BF16),
            pltpu.VMEM((heads_width // 128, width, 256), BF16),
            pltpu.VMEM((width, heads_width), BF16),
            pltpu.VMEM((4 * heads_width, width // 2), BF16),
            pltpu.VMEM((rows, heads_width), BF16),
            pltpu.VMEM((rows, 4 * heads_width), BF16),
            pltpu.VMEM((rows, 4 * heads_width), BF16),
            kv, kv, kv, kv, kv, kv,
            pltpu.VMEM((frame, 256), BF16),
            pltpu.VMEM((rows, width // 4), BF16),
            pltpu.VMEM((3, level_count, width), F32),
            pltpu.VMEM((2, 8, width), F32),
            pltpu.VMEM((8, width), F32),
            pltpu.SemaphoreType.DMA((10,)),
            pltpu.SemaphoreType.DMA((N_SEM,)),
            pltpu.SemaphoreType.DMA((N_SEM,)),
        ],
        compiler_params=pltpu.CompilerParams(
            collective_id=0, has_side_effects=True, vmem_limit_bytes=60 * 1024 * 1024
        ),
        cost_estimate=pl.CostEstimate(
            flops=4 * rows * width * 1536 * 2, bytes_accessed=40 * 2**20, transcendentals=10**7
        ),
    )(
        queue_latents.reshape(rows, width),
        fresh_noise,
        levels,
        window_start,
        jnp.transpose(modulation, (1, 0, 2)),
        jnp.transpose(w_qkv, (1, 0, 2)),
        qk_gain,
        w_out,
        jnp.transpose(sampler, (1, 0)),
    )
    return result.reshape(frames, frame, width)


def solution(mesh):
    in_specs = (
        P("queue", None, None),
        P(),
        P("queue"),
        P("queue"),
        P(),
        P(None, None, "tensor"),
        P(None, "tensor"),
        P("tensor", None),
        P(),
    )
    out_specs = P("queue", None, None)
    return jax.shard_map(body, mesh=mesh, in_specs=in_specs, out_specs=out_specs, check_vma=False)
```

time: 587 us -> 213 us (0.36)
  the two profiles are of different devices: /device:TPU:102 before, /device:TPU:111 now
where the time goes in v1:
time: 213 us; the launch traced here: 212 us
  Pallas kernels  208 us (98%)
  local copies, waits for them, and re-layouts  4.84 us (2%)
    pallas_call x1, Pallas kernels, body(): pl.pallas_call(functools.partial(kernel, frame, width, heads_width), name...  208 us
    unnamed x1, local copies, waits for them, and re-layouts  4.84 us

profile of v1, /device:TPU:111, one launch (start us, length us, event | category | flops | bytes accessed | tf_op | source)
XLA Modules:
  0.0 212.4 jit_solution(1367249425703202677)
XLA Ops:
  0.0 207.5 %diagonal_steps.1 = bf16[768,3072]{1,0:T(8,128)(2,1)} custom-call(bf16[768,3072]{1,0:T(8,128)(2,1)} %bitcast.7, bf16[2,384,3072]{2,1,0:T(8,128)(2,1)} %fresh.1, s32[2]{0:T(128)} %levels.1, s32[2]{0:T(128)} %window_start.1, f32[3,50,3072]{2,1,0:T(8,128)} %bitcast.8, bf16[3,3072,384]{2,1,0:T(8,128)(2,1)} %bitcast.6, f32[2,384]{1,0:T(2,128)} %gain.1, ...), custom_call_target="tpu_custom_call" | custom-call | flops 28991029248 | bytes 41943040 | tf_op jit(solution)/shard_map/diagonal_steps/pallas_call | solution.py:476
  207.5 4.8 %copy.11 = bf16[2,384,3072]{2,1,0:T(8,128)(2,1)} copy(bf16[2,384,3072]{2,1,0:T(8,128)(2,1)} %bitcast.5) | data formatting | bytes 9437184

commit v2 on v1

--- a/solution.py
+++ b/solution.py
@@ -24,17 +24,17 @@
 slots("halo_up", 6)
 slots("halo_down", 6)
 slots("halo_wrap", 3)
-slots("attn_core", 6)
-slots("attn_y", 6)
-slots("attn_fwd", 6)
+slots("attn_core", 12)
+slots("attn_y", 12)
+slots("attn_fwd", 12)
 slots("wout_core", 1)
 slots("wout_y", 4)
 slots("wout_x", 4)
 slots("gather", 6)
-slots("shift", 4)
-slots("out_y", 4)
-slots("out_core", 4)
-slots("out_fwd", 4)
+slots("shift", 8)
+slots("out_y", 8)
+slots("out_core", 8)
+slots("out_fwd", 8)
 slots("meta", 1)
 N_SEM = sum(n for _, n in SEM.values())
 
@@ -44,7 +44,7 @@
     x_in, fresh, levels, window_start, mod_in, w_in, gain, wout_in, sampler,
     out,
     x0, x1, h, wkv, wq, wfull, q, attn0, attn1, kv00, kv01, kv02, kv10, kv11, kv12,
-    chosen, xs, mod, slot0, slot1, lsem, ssem, rsem,
+    xs, mod, slot0, slot1, lsem, ssem, rsem,
 ):
     rows = 2 * frame
     half = width // 2
@@ -87,10 +87,13 @@
     def at_row(start, size):
         return pl.ds(pl.multiple_of(start, 16), size)
 
-    load_x = local(0, x_in, x0)
     load_mod = local(1, mod_in, mod)
-    load_x.start()
     load_mod.start()
+    load_x = []
+    for f, index in ((0, 0), (1, 11)):
+        at = slice(f * frame, (f + 1) * frame)
+        load_x.append(local(index, x_in.at[at], x0.at[at]))
+        load_x[f].start()
     load_w = []
     for p in range(pairs):
         for j in (1, 2):
@@ -99,12 +102,15 @@
                       wkv.at[p, :, (j - 1) * 128 : j * 128])
             )
     load_w.append(local(8, w_in.at[0], wq))
-    for load in load_w:
-        load.start()
     my_half = at_lane(core * half, half)
     other_half = at_lane((1 - core) * half, half)
     load_wout = local(9, wout_in.at[:, my_half], wfull.at[at_row(ti * heads_width, heads_width)])
-    load_wout.start()
+
+    last = local(10, fresh.at[1], out.at[frame:rows])
+
+    @pl.when(final)
+    def _():
+        last.start()
 
     barrier = pltpu.get_barrier_semaphore()
     partners = [
@@ -187,94 +193,93 @@
             slot0[f, j : j + 1, :] = mod[j, pl.ds(levels[f], 1), :]
     send("meta", 0, slot0.at[1], slot1, (up, ti))
 
-    def norm_rows(src, params):
-        chunk = 16
+    def norm_rows(src, params, f):
+        param = params[f]
+        chunk = 64
+
+        @pl.loop(0, frame // chunk)
+        def _(i):
+            at = pl.ds(pl.multiple_of(f * frame + i * chunk, chunk), chunk)
+            mean = jnp.mean(src[at, :].astype(F32), axis=-1, keepdims=True)
+            centered = src[at, :].astype(F32) - mean
+            var = jnp.mean(centered * centered, axis=-1, keepdims=True)
+            normed = (src[at, :].astype(F32) - mean) * lax.rsqrt(var + EPS)
+            h[at, :] = (normed * (1.0 + param[1:2, :]) + param[0:1, :]).astype(BF16)
+
+    def project_kv(kv, p):
+        acc = jnp.dot(h[...], wkv[p], preferred_element_type=F32)
         for f in range(2):
-            param = params[f]
-
-            @pl.loop(0, frame // chunk)
-            def _(i):
-                at = pl.ds(pl.multiple_of(f * frame + i * chunk, chunk), chunk)
-                values = src[at, :].astype(F32)
-                mean = jnp.mean(values, axis=-1, keepdims=True)
-                centered = values - mean
-                var = jnp.mean(centered * centered, axis=-1, keepdims=True)
-                normed = centered * lax.rsqrt(var + EPS)
-                h[at, :] = (
-                    normed * (1.0 + param[1:2, :]) + param[0:1, :]
-                ).astype(BF16)
-
-    def project_kv(kv, p):
-        @pl.loop(0, 2)
-        def _(f):
-            at = pl.ds(pl.multiple_of(f * frame, frame), frame)
-            acc = jnp.dot(h[at, :], wkv[p], preferred_element_type=F32)
-            kv[f + 2, :, 0:128] = head_norm(acc[:, :128], gain[1:2, p * 128 : (p + 1) * 128])
-            kv[f + 2, :, 128:256] = acc[:, 128:].astype(BF16)
+            part = acc[f * frame : (f + 1) * frame]
+            kv[f + 2, :, 0:128] = head_norm(part[:, :128], gain[1:2, p * 128 : (p + 1) * 128])
+            kv[f + 2, :, 128:256] = part[:, 128:].astype(BF16)
 
     def project_q():
-        @pl.loop(0, 2)
-        def _(f):
-            at = pl.ds(pl.multiple_of(f * frame, frame), frame)
-            acc = jnp.dot(h[at, :], wq[...], preferred_element_type=F32)
-            for p in range(pairs):
-                cols = slice(p * 128, (p + 1) * 128)
-                q[at, cols] = head_norm(acc[:, cols], gain[0:1, cols]) * jnp.asarray(0.125, BF16)
-
-    q_chunk = frame // 2
+        acc = jnp.dot(h[...], wq[...], preferred_element_type=F32)
+        for p in range(pairs):
+            cols = slice(p * 128, (p + 1) * 128)
+            q[:, cols] = head_norm(acc[:, cols], gain[0:1, cols]) * jnp.asarray(0.125, BF16)
+
+    q_chunk = 128
     first_head = lax.broadcasted_iota(jnp.int32, (q_chunk, 128), 1) < 64
     zeros = jnp.zeros((q_chunk, 128), BF16)
     ones = jnp.ones((WIN * frame, 128), BF16)
 
     def attend(kv, p, f, window, flag, attn):
         fixed, second, if_set, if_clear = window
-        chosen[...] = jnp.where(
-            flag, kv[if_set].astype(F32), kv[if_clear].astype(F32)
-        ).astype(BF16)
-
-        @pl.loop(0, 2)
-        def _(i):
-            at = pl.ds(pl.multiple_of(f * frame + i * q_chunk, 16), q_chunk)
-            keys = jnp.concatenate(
-                [kv[fixed, :, 0:128], kv[second, :, 0:128], chosen[:, 0:128]], axis=0
-            )
-            values = jnp.concatenate(
-                [kv[fixed, :, 128:256], kv[second, :, 128:256], chosen[:, 128:256]], axis=0
-            )
-            values = jnp.concatenate([values, ones], axis=1)
-            rows_q = q[at, p * 128 : (p + 1) * 128]
+        chosen = jnp.where(flag, kv[if_set].astype(F32), kv[if_clear].astype(F32)).astype(BF16)
+        keys = jnp.concatenate([kv[fixed, :, 0:128], kv[second, :, 0:128], chosen[:, 0:128]], axis=0)
+        values = jnp.concatenate(
+            [kv[fixed, :, 128:256], kv[second, :, 128:256], chosen[:, 128:256]], axis=0
+        )
+        values = jnp.concatenate([values, ones], axis=1)
+
+        def scores_of(i):
+            start = f * frame + i * q_chunk
+            rows_q = q[start : start + q_chunk, p * 128 : (p + 1) * 128]
             both = jnp.concatenate(
                 [jnp.where(first_head, rows_q, zeros), jnp.where(first_head, zeros, rows_q)], axis=0
             )
-            scores = lax.dot_general(
+            return lax.dot_general(
                 both, keys, (((1,), (1,)), ((), ())), preferred_element_type=F32
             )
+
+        n = frame // q_chunk
+        ahead = scores_of(0)
+        for i in range(n):
+            scores = ahead
+            if i + 1 < n:
+                ahead = scores_of(i + 1)
             top = jnp.max(scores, axis=-1, keepdims=True)
             expo = jnp.exp(scores - top).astype(BF16)
             total = jnp.dot(expo, values, preferred_element_type=F32)
-            mixed = total[:, :128] / total[:, 128:]
-            attn[at, at_lane(ti * heads_width + p * 128, 128)] = jnp.where(
-                first_head, mixed[:q_chunk], mixed[q_chunk:]
+            picked = jnp.where(
+                jnp.concatenate([first_head, first_head], axis=1), total[:q_chunk], total[q_chunk:]
+            )
+            start = f * frame + i * q_chunk
+            attn[start : start + q_chunk, at_lane(ti * heads_width + p * 128, 128)] = (
+                picked[:, :128] / picked[:, 128:]
             ).astype(BF16)
 
-    def attn_block(attn, t, p):
-        return attn.at[:, at_lane(t * heads_width + p * 128, 128)]
-
-    def share_attn(step, attn, p):
-        mine = attn_block(attn, ti, p)
-        send("attn_core", step * 3 + p, mine, mine, (qi, t_core))
-        send("attn_y", step * 3 + p, mine, mine, (qi, t_y))
-
-    def forward_attn(step, attn, p):
-        block = attn_block(attn, t_y, p)
-        landed("attn_y", step * 3 + p, block)
-        send("attn_fwd", step * 3 + p, block, block, (qi, t_core))
-
-    def finish_attn(step, attn):
+    def attn_block(attn, t, p, f):
+        return attn.at[f * frame : (f + 1) * frame, at_lane(t * heads_width + p * 128, 128)]
+
+    def attn_slot(step, p, f):
+        return step * 6 + p * 2 + f
+
+    def share_attn(step, attn, p, f):
+        mine = attn_block(attn, ti, p, f)
+        send("attn_y", attn_slot(step, p, f), mine, mine, (qi, t_y))
+        send("attn_core", attn_slot(step, p, f), mine, mine, (qi, t_core))
+
+    def forward_attn(step, attn, p, f):
+        block = attn_block(attn, t_y, p, f)
+        landed("attn_y", attn_slot(step, p, f), block)
+        send("attn_fwd", attn_slot(step, p, f), block, block, (qi, t_core))
+
+    def finish_attn(step, attn, f):
         for p in range(pairs):
-            landed("attn_core", step * 3 + p, attn_block(attn, t_core, p))
-        for p in range(pairs):
-            landed("attn_fwd", step * 3 + p, attn_block(attn, t_far, p))
+            landed("attn_core", attn_slot(step, p, f), attn_block(attn, t_core, p, f))
+            landed("attn_fwd", attn_slot(step, p, f), attn_block(attn, t_far, p, f))
 
     def update(values, branch, param, columns):
         values = values.astype(F32)
@@ -298,8 +303,12 @@
         start = jnp.concatenate([param[5:6, 0:128]] * 2, axis=1)
         return start >= slot.astype(F32)
 
-    load_x.wait()
-    norm_rows(x0, param0)
+    for f in range(2):
+        load_x[f].wait()
+        if f == 1:
+            for load in load_w + [load_wout]:
+                load.start()
+        norm_rows(x0, param0, f)
     for p in range(pairs):
         load_w[2 * p].wait()
         load_w[2 * p + 1].wait()
@@ -323,12 +332,14 @@
 
         for f in range(2):
             attend(kv0[p], p, f, window0[f], starts_from(param0[f], 2 * qi - 1 + 2 * f), attn0)
-        share_attn(0, attn0, p)
-        if p > 0:
-            forward_attn(0, attn0, p - 1)
-    forward_attn(0, attn0, pairs - 1)
+            share_attn(0, attn0, p, f)
+            if p > 0:
+                forward_attn(0, attn0, p - 1, f)
     finish_wout()
-    finish_attn(0, attn0)
+    for f in range(2):
+        forward_attn(0, attn0, pairs - 1, f)
+    for f in range(2):
+        finish_attn(0, attn0, f)
 
     n_cols = 256
 
@@ -356,7 +367,8 @@
         entered.wait()
 
     landed("meta", 0, slot1)
-    norm_rows(x1, param1)
+    for f in range(2):
+        norm_rows(x1, param1, f)
     for p in range(pairs):
         project_kv(kv1[p], p)
         send("halo_up", 3 + p, kv1[p].at[3], kv1[p].at[1], (up, ti))
@@ -373,13 +385,11 @@
 
         for f in range(2):
             attend(kv1[p], p, f, window1[f], starts_from(param1[f], 2 * qi - 1), attn1)
-        share_attn(1, attn1, p)
-        if p > 0:
-            forward_attn(1, attn1, p - 1)
-    forward_attn(1, attn1, pairs - 1)
-    finish_attn(1, attn1)
-
-    chunks = 4
+            share_attn(1, attn1, p, f)
+            if p > 0:
+                forward_attn(1, attn1, p - 1, f)
+
+    chunks = 8
     n_rows = rows // chunks
     my_quarter = core * half + chip * quarter
     y_quarter = core * half + (1 - chip) * quarter
@@ -387,9 +397,10 @@
     def out_part(j, start):
         return out.at[at_row(j * n_rows, n_rows), at_lane(start, quarter)]
 
-    for j in range(chunks):
-        f = j // 2
-        at = slice(j * n_rows, (j + 1) * n_rows)
+    for f in range(2):
+        forward_attn(1, attn1, pairs - 1, f)
+        finish_attn(1, attn1, f)
+        at = slice(f * frame, (f + 1) * frame)
 
         @pl.loop(0, quarter // n_cols)
         def _(n):
@@ -399,17 +410,12 @@
             branch = jnp.dot(attn1[at, :], weight, preferred_element_type=F32)
             xs[at, inner] = update(x1[at, columns], branch, param1[f], columns)
 
-        part = (xs.at[at], out_part(j, my_quarter), (down, ti))
-        if f == 0:
-            send("shift", j, *part)
-        else:
-            send_if(jnp.logical_not(first), "shift", j, *part)
-
-    @pl.when(final)
-    def _():
-        last = local(0, fresh.at[1], out.at[frame:rows])
-        last.start()
-        last.wait()
+        for j in range(f * chunks // 2, (f + 1) * chunks // 2):
+            part = (xs.at[j * n_rows : (j + 1) * n_rows], out_part(j, my_quarter), (down, ti))
+            if f == 0:
+                send("shift", j, *part)
+            else:
+                send_if(jnp.logical_not(first), "shift", j, *part)
 
     def guarded(f, action):
         if f == 0:
@@ -424,7 +430,7 @@
             rcopy("out_y", j, part, part, (qi, t_y)).start()
             rcopy("out_core", j, part, part, (qi, t_core)).start()
 
-        guarded(j // 2, action)
+        guarded(j // (chunks // 2), action)
 
     def pass_on(j):
         def action():
@@ -432,7 +438,7 @@
             landed("out_y", j, part)
             rcopy("out_fwd", j, part, part, (qi, t_core)).start()
 
-        guarded(j // 2, action)
+        guarded(j // (chunks // 2), action)
 
     for j in range(chunks):
         spread(j)
@@ -453,7 +459,11 @@
             passed = out_part(j, y_quarter)
             rcopy("out_fwd", j, passed, passed, (qi, t_core)).wait_send()
 
-        guarded(j // 2, action)
+        guarded(j // (chunks // 2), action)
+
+    @pl.when(final)
+    def _():
+        last.wait()
 
     for cond, copy in sends:
         if cond is None:
@@ -490,12 +500,11 @@
             pltpu.VMEM((rows, 4 * heads_width), BF16),
             pltpu.VMEM((rows, 4 * heads_width), BF16),
             kv, kv, kv, kv, kv, kv,
-            pltpu.VMEM((frame, 256), BF16),
             pltpu.VMEM((rows, width // 4), BF16),
             pltpu.VMEM((3, level_count, width), F32),
             pltpu.VMEM((2, 8, width), F32),
             pltpu.VMEM((8, width), F32),
-            pltpu.SemaphoreType.DMA((10,)),
+            pltpu.SemaphoreType.DMA((12,)),
             pltpu.SemaphoreType.DMA((N_SEM,)),
             pltpu.SemaphoreType.DMA((N_SEM,)),
         ],

time: 213 us -> 157 us (0.74)
  the two profiles are of different devices: /device:TPU:111 before, /device:TPU:15 now
where the time goes in v2:
time: 157 us
  Pallas kernels  152 us (97%)
  local copies, waits for them, and re-layouts  4.84 us (3%)
    pallas_call x1, Pallas kernels, body(): pl.pallas_call(functools.partial(kernel, frame, width, heads_width), name...  152 us
    unnamed x1, local copies, waits for them, and re-layouts  4.84 us

profile of v2, /device:TPU:15, one launch (start us, length us, event | category | flops | bytes accessed | tf_op | source)
XLA Modules:
  0.0 157.2 jit_solution(5275103982818082287)
XLA Ops:
  0.0 152.4 %diagonal_steps.1 = bf16[768,3072]{1,0:T(8,128)(2,1)} custom-call(bf16[768,3072]{1,0:T(8,128)(2,1)} %bitcast.7, bf16[2,384,3072]{2,1,0:T(8,128)(2,1)} %fresh.1, s32[2]{0:T(128)} %levels.1, s32[2]{0:T(128)} %window_start.1, f32[3,50,3072]{2,1,0:T(8,128)} %bitcast.8, bf16[3,3072,384]{2,1,0:T(8,128)(2,1)} %bitcast.6, f32[2,384]{1,0:T(2,128)} %gain.1, ...), custom_call_target="tpu_custom_call" | custom-call | flops 28991029248 | bytes 41943040 | tf_op jit(solution)/shard_map/diagonal_steps/pallas_call | solution.py:486
  152.4 4.8 %copy.11 = bf16[2,384,3072]{2,1,0:T(8,128)(2,1)} copy(bf16[2,384,3072]{2,1,0:T(8,128)(2,1)} %bitcast.5) | data formatting | bytes 9437184
